TPU v7x, 32 devices: a whole 2x2x4 slice. The times are simulated.
32 devices in a mesh: lat: 2 (over x), lon: 16 (over z, y, core).
Axes of the slice: x: 2, y: 2, z: 4, core: 2. Of those that a mesh axis runs over, the one named last changes fastest.
Arguments:
- stream: bfloat16 [2, 48, 48, 768], P(None, 'lat', 'lon'), may hold values from -6 to 6
- land: int32 [48, 48], P('lat', 'lon'), may hold values from 0 to 16
- orography: int32 [48, 48], P('lat', 'lon'), may hold values from 0 to 7
- land_vector: float32 [768], replicated, may hold values from -6 to 6
- orography_table: float32 [8, 768], replicated, may hold values from -6 to 6
- gain_one: float32 [768], replicated, may hold values from 0.1 to 1.9
- qkv_one: bfloat16 [768, 2304], replicated, may hold values from -0.21875 to 0.21875
- proj_one: bfloat16 [768, 768], replicated, may hold values from -0.875 to 0.875
- table_one: bfloat16 [4, 12, 6336], P('lat'), may hold values from -4 to 250
- gain_two: float32 [768], replicated, may hold values from 0.1 to 1.9
- qkv_two: bfloat16 [768, 2304], replicated, may hold values from -0.21875 to 0.21875
- proj_two: bfloat16 [768, 768], replicated, may hold values from -0.875 to 0.875
- table_two: bfloat16 [4, 12, 6336], P('lat'), may hold values from -4 to 250
- cotangent: bfloat16 [2, 48, 48, 768], P(None, 'lat', 'lon'), may hold values from -6 to 6
Outputs:
- output: bfloat16 [2, 48, 48, 768], P(None, 'lat', 'lon')
- grad_stream: bfloat16 [2, 48, 48, 768], P(None, 'lat', 'lon')
All inputs are finite; a program needn't handle non-finite values.
Results may differ from a plain program's by a relative error of at most 0.027.
Values may be sent and summed in bfloat16 or wider, within the bound.
A program may use at most 192 MiB of HBM per device.

v0:
```python
import jax
import jax.numpy as jnp
from jax import lax
from jax.sharding import PartitionSpec as P

WZ = 2
WLAT = 12
WLON = 6
OROG = 8
LAND = 16


epsilon = 1e-05
highest = lax.Precision.HIGHEST


def shifted_2(value, axis, steps):
    count = lax.axis_size(axis)
    pairs = [(source, (source + steps) % count) for source in range(count)]
    return lax.ppermute(value, axis, pairs)


def from_partner(value, axis, bit):
    return lax.ppermute(value, axis, [(i, i ^ 1 << bit) for i in range(lax.axis_size(axis))])


def layer_norm(stream, gain):
    values = stream.astype(jnp.float32)
    average = jnp.mean(values, axis=-1, keepdims=True)
    centred = values - average
    inverse = lax.rsqrt(jnp.mean(centred * centred, axis=-1, keepdims=True) + epsilon)
    normed = centred * inverse
    return ((normed * gain).astype(jnp.bfloat16), normed, inverse)


def norm_back(grad_normed_in, normed, inverse, gain):
    scaled = grad_normed_in * gain
    first = jnp.mean(scaled, axis=-1, keepdims=True)
    second = jnp.mean(scaled * normed, axis=-1, keepdims=True)
    return (scaled - first - normed * second) * inverse


def window_bias_part(table, first, count):
    heads = table.shape[0]
    shaped = table.astype(jnp.float32).reshape(heads, WZ, WZ, WLAT, WLAT, 2 * WLON - 1)
    query_col = first + jnp.arange(count, dtype=jnp.int32)
    key_col = jnp.arange(WLON, dtype=jnp.int32)
    offset = query_col[:, None] - key_col[None, :] + (WLON - 1)
    picked = jnp.take(shaped, offset, axis=5)
    picked = picked.transpose(0, 1, 3, 5, 2, 4, 6)
    return picked.reshape(heads, WZ, WLAT, count, WZ * WLAT * WLON)


def to_heads(array, heads, groups):
    levels, rows, width, chans = array.shape
    depth = chans // (groups * heads)
    windows = rows // WLAT
    shaped = array.reshape(levels, windows, WLAT, width, groups, heads, depth)
    shaped = shaped.transpose(4, 1, 5, 0, 2, 3, 6)
    return shaped.reshape(groups, windows, heads, levels * WLAT * width, depth)


def from_heads(array, levels, width):
    groups, windows, heads, tokens, depth = array.shape
    shaped = array.reshape(groups, windows, heads, levels, WLAT, width, depth)
    shaped = shaped.transpose(3, 1, 4, 5, 0, 2, 6)
    return shaped.reshape(levels, windows * WLAT, width, groups * heads * depth)


def pair_mask(row_start, rows, total_rows, width):
    line = row_start + jnp.arange(rows, dtype=jnp.int32)
    upper = (line >= total_rows - WLAT // 2).reshape(rows // WLAT, 1, WLAT, 1)
    query_side = jnp.broadcast_to(upper, (rows // WLAT, WZ, WLAT, width)).reshape(rows // WLAT, -1)
    key_side = jnp.broadcast_to(upper, (rows // WLAT, WZ, WLAT, 2 * width)).reshape(
        rows // WLAT, -1
    )
    return query_side[:, :, None] == key_side[:, None, :]


def attend(queries, keys, values, bias, allowed):
    scale = queries.shape[-1] ** (-0.5)
    scores = (
        jnp.einsum("whqe,whke->whqk", queries, keys, preferred_element_type=jnp.float32) * scale
        + bias
    )
    if allowed is not None:
        scores = jnp.where(allowed[:, None], scores, -1000000000.0)
    largest = jnp.max(scores, axis=-1, keepdims=True)
    expo = jnp.exp(scores - largest)
    probs = expo / jnp.sum(expo, axis=-1, keepdims=True)
    rounded = probs.astype(jnp.bfloat16)
    mixed = jnp.einsum("whqk,whke->whqe", rounded, values, preferred_element_type=jnp.float32)
    return (mixed.astype(jnp.bfloat16), probs, rounded)


def attend_back(queries, keys, values, probs, rounded, grad_mixed):
    scale = queries.shape[-1] ** (-0.5)
    grad_probs = jnp.einsum(
        "whqe,whke->whqk", grad_mixed, values, preferred_element_type=jnp.float32
    )
    inner = jnp.sum(probs * grad_probs, axis=-1, keepdims=True)
    grad_scores = (probs * (grad_probs - inner) * scale).astype(jnp.bfloat16)
    grad_q = jnp.einsum("whqk,whke->whqe", grad_scores, keys, preferred_element_type=jnp.float32)
    grad_k = jnp.einsum("whqk,whqe->whke", grad_scores, queries, preferred_element_type=jnp.float32)
    grad_v = jnp.einsum("whqk,whqe->whke", rounded, grad_mixed, preferred_element_type=jnp.float32)
    return (grad_q, grad_k.astype(jnp.bfloat16), grad_v.astype(jnp.bfloat16))


def move_columns(field, offset):
    return shifted_2(field, "lon", offset)


def move_rows(field, offset):
    return shifted_2(field, "lat", offset)


def roll_field(field, sign):
    half = WLAT // 2
    rows = field.shape[1]
    if sign < 0:
        moved = move_columns(field, -1)
        strip = move_rows(moved[:, :half], -1)
        return jnp.concatenate([moved[:, half:], strip], axis=1)
    strip = move_rows(field[:, rows - half :], 1)
    settled = jnp.concatenate([strip, field[:, : rows - half]], axis=1)
    return move_columns(settled, 1)


def block_forward(stream, gain, weight_qkv, weight_proj, table, allowed, parity):
    levels, rows, width, dims = stream.shape
    heads = table.shape[1]
    windows = rows // WLAT
    normed_in, normed, inverse = layer_norm(stream, gain)
    projected = jnp.dot(normed_in.reshape(-1, dims), weight_qkv, preferred_element_type=jnp.float32)
    projected = projected.astype(jnp.bfloat16).reshape(levels, rows, width, 3 * dims)
    near = projected[..., dims:]
    far = from_partner(near, "lon", 0)
    pairs = jnp.where(
        parity == 0, jnp.concatenate([near, far], axis=2), jnp.concatenate([far, near], axis=2)
    )
    queries = to_heads(projected[..., :dims], heads, 1)[0]
    key_values = to_heads(pairs, heads, 2)
    keys = key_values[0]
    values = key_values[1]
    first_col = parity * width

    def bias_of(one_table):
        return window_bias_part(one_table, first_col, width)

    bias = jax.vmap(bias_of)(table)
    bias = bias.reshape(windows, heads, -1, bias.shape[-1])
    mixed, probs, rounded = attend(queries, keys, values, bias, allowed)
    mixed_rows = from_heads(mixed[None], levels, width)
    added = jnp.dot(
        mixed_rows.reshape(-1, dims), weight_proj, preferred_element_type=jnp.float32
    ).reshape(stream.shape)
    result = (stream.astype(jnp.float32) + added).astype(jnp.bfloat16)
    return (result, (normed, inverse, queries, keys, values, probs, rounded))


def block_backward(grad, saved, gain, weight_qkv, weight_proj, parity):
    normed, inverse, queries, keys, values, probs, rounded = saved
    levels, rows, width, dims = grad.shape
    heads = queries.shape[1]
    grad_mixed = jnp.dot(grad.reshape(-1, dims), weight_proj.T, preferred_element_type=jnp.float32)
    grad_mixed = grad_mixed.astype(jnp.bfloat16).reshape(grad.shape)
    grad_windows = to_heads(grad_mixed, heads, 1)[0]
    grad_q, grad_k, grad_v = attend_back(queries, keys, values, probs, rounded, grad_windows)
    key_grads = from_heads(jnp.stack([grad_k, grad_v]), levels, 2 * width)
    lower = key_grads[:, :, :width]
    upper = key_grads[:, :, width:]
    own = jnp.where(parity == 0, lower, upper)
    other = jnp.where(parity == 0, upper, lower)
    received = from_partner(other, "lon", 0)
    summed = (own.astype(jnp.float32) + received.astype(jnp.float32)).astype(jnp.bfloat16)
    query_grads = from_heads(grad_q[None], levels, width).astype(jnp.bfloat16)
    grad_qkv = jnp.concatenate([query_grads, summed], axis=-1)
    grad_normed_in = jnp.dot(
        grad_qkv.reshape(-1, 3 * dims), weight_qkv.T, preferred_element_type=jnp.float32
    ).reshape(grad.shape)
    return (grad.astype(jnp.float32) + norm_back(grad_normed_in, normed, inverse, gain)).astype(
        jnp.bfloat16
    )


def body(
    stream,
    land,
    orography,
    land_vector,
    orography_table,
    gain_one,
    qkv_one,
    proj_one,
    table_one,
    gain_two,
    qkv_two,
    proj_two,
    table_two,
    cotangent,
):
    levels, rows, width, dims = stream.shape
    parity = lax.axis_index("lon") % 2
    first_row = lax.axis_index("lat") * rows
    total_rows = rows * lax.axis_size("lat")
    onehot = (orography[..., None] == jnp.arange(OROG, dtype=jnp.int32)).astype(jnp.float32)
    looked = jnp.dot(onehot.reshape(-1, OROG), orography_table, precision=highest).reshape(
        rows, width, dims
    )
    added = (land.astype(jnp.float32) / LAND)[..., None] * land_vector + looked
    embedded = (stream.astype(jnp.float32) + added[None]).astype(jnp.bfloat16)
    shifted = pair_mask(first_row, rows, total_rows, width)
    middle, saved_one = block_forward(
        embedded, gain_one, qkv_one, proj_one, table_one, None, parity
    )
    turned, saved_two = block_forward(
        roll_field(middle, -1), gain_two, qkv_two, proj_two, table_two, shifted, parity
    )
    output = roll_field(turned, 1)
    grad_turned = block_backward(
        roll_field(cotangent, -1), saved_two, gain_two, qkv_two, proj_two, parity
    )
    grad_stream = block_backward(
        roll_field(grad_turned, 1), saved_one, gain_one, qkv_one, proj_one, parity
    )
    return (output, grad_stream)


def solution(mesh):
    placed = (
        P(None, "lat", "lon", None),
        P("lat", "lon"),
        P("lat", "lon"),
        P(),
        P(),
        P(),
        P(),
        P(),
        P("lat", None, None),
        P(),
        P(),
        P(),
        P("lat", None, None),
        P(None, "lat", "lon", None),
    )
    return jax.shard_map(
        body,
        mesh=mesh,
        in_specs=placed,
        out_specs=(P(None, "lat", "lon", None), P(None, "lat", "lon", None)),
        check_vma=False,
    )
```

profile of v0, /device:TPU:1, one launch (start us, length us, event | category | flops | bytes accessed | tf_op | source)
XLA Modules:
  0.0 523.6 jit_solution(17534838452650221128)
XLA Ops:
  8.6 3.7 convolution_convert_fusion.1
  16.8 7.1 %reshape.222 = f32[2,12,2,2,12,12,11]{6,5,4,3,2,0,1:T(8,128)} reshape(bf16[2,12,6336]{2,0,1:T(2,128)(2,1)} %param.28) | data formatting | bytes 912384 | tf_op jit(solution)/shard_map/vmap()/reshape | solution.py:45
  23.9 13.5 %copy.121 = f32[2,12,2,2,12,12,11]{5,4,3,2,1,0,6:T(8,128)} copy(f32[2,12,2,2,12,12,11]{6,5,4,3,2,0,1:T(8,128)} %reshape.222) | data formatting | bytes 1216512 | tf_op jit(solution)/shard_map/vmap()/reshape | solution.py:45
  37.4 11.9 %gather_fusion.1 = f32[18,2,12,2,2,12,12]{6,5,4,3,2,1,0:T(8,128)} fusion(f32[2,12,2,2,12,12,11]{5,4,3,2,1,0,6:T(8,128)} %copy.121, s32[1024]{0:T(1024)S(1)} %pad_clamp_fusion), kind=kCustom, calls=%fused_computation.1.clone | custom fusion | bytes 1990728 | tf_op jit(solution)/shard_map/vmap(jit(_take))/gather | solution.py:49
  49.3 16.3 %copy.122 = f32[18,2,12,2,2,12,12]{6,4,5,3,2,1,0:T(2,128)} copy(f32[18,2,12,2,2,12,12]{6,5,4,3,2,1,0:T(8,128)} %gather_fusion.1) | data formatting | bytes 1990656 | tf_op jit(solution)/shard_map/vmap(jit(_take))/gather | solution.py:49
  65.6 7.1 %reshape.219 = f32[2,12,2,2,12,12,11]{6,5,4,3,2,0,1:T(8,128)} reshape(bf16[2,12,6336]{2,0,1:T(2,128)(2,1)} %param.24) | data formatting | bytes 912384 | tf_op jit(solution)/shard_map/vmap()/reshape | solution.py:45
  72.7 13.5 %copy.103 = f32[2,12,2,2,12,12,11]{5,4,3,2,1,0,6:T(8,128)} copy(f32[2,12,2,2,12,12,11]{6,5,4,3,2,0,1:T(8,128)} %reshape.219) | data formatting | bytes 1216512 | tf_op jit(solution)/shard_map/vmap()/reshape | solution.py:45
  86.2 11.9 %gather_fusion = f32[18,2,12,2,2,12,12]{6,5,4,3,2,1,0:T(8,128)} fusion(f32[2,12,2,2,12,12,11]{5,4,3,2,1,0,6:T(8,128)} %copy.103, s32[1024]{0:T(1024)S(1)} %pad_clamp_fusion), kind=kCustom, calls=%fused_computation.clone | custom fusion | bytes 1990728 | tf_op jit(solution)/shard_map/vmap(jit(_take))/gather | solution.py:49
  98.1 15.5 %copy.104 = f32[18,2,12,2,2,12,12]{6,4,5,3,2,1,0:T(2,128)S(1)} copy(f32[18,2,12,2,2,12,12]{6,5,4,3,2,1,0:T(8,128)} %gather_fusion) | data formatting | bytes 1990656 | tf_op jit(solution)/shard_map/vmap(jit(_take))/gather | solution.py:49
  113.6 14.2 %select_bitcast_fusion = (f32[2,12,2,12,3,2,12,6]{6,5,3,2,1,0,7,4:T(2,128)}, f32[2,12,2,12,3,2,12,6]{6,5,3,2,1,0,7,4:T(2,128)}) fusion(f32[3,6,2,12,2,2,12,12]{7,5,6,4,3,2,1,0:T(2,128)} %bitcast.154, pred[3,6]{1,0:T(4,128)(4,1)S(1)} %compare_and_fusion, f32[3,6,2,12,2,2,12,12]{7,5,6,4,3,2,1,0:T(2,128)S(1)} %bitcast.155), kind=kLoop, calls=%fused_computation.6 | loop fusion | flops 497664 | bytes 3981330 | tf_op jit(solution)/shard_map/vmap()/transpose | solution.py:50
  132.3 24.1 %copy.105 = f32[2,12,2,12,3,2,12,6]{1,0,7,6,5,4,3,2:T(2,128)} copy(f32[2,12,2,12,3,2,12,6]{6,5,3,2,1,0,7,4:T(2,128)} %get-tuple-element.14) | data formatting | bytes 1990656 | tf_op jit(solution)/shard_map/vmap()/transpose | solution.py:50
  156.5 15.4 %copy.106 = f32[2,12,72,144]{3,2,1,0:T(8,128)} copy(f32[2,12,72,144]{1,0,3,2:T(2,128)} %bitcast.152) | data formatting | bytes 1990656 | tf_op jit(solution)/shard_map/reshape;vmap()/reshape | solution.py:151
  182.5 3.6 fusion.8
  198.8 13.8 %copy.108 = bf16[2,12,144,64]{2,3,1,0:T(8,128)(2,1)} copy(bf16[2,12,144,64]{3,0,2,1:T(2,128)(2,1)} %bitcast.161) | data formatting | bytes 884736 | tf_op jit(solution)/shard_map/squeeze | solution.py:144
  212.7 6.1 %convolution_convert_fusion.5 = bf16[2,12,72,64]{2,3,1,0:T(8,128)(2,1)} fusion(bf16[2,12,144,64]{2,3,1,0:T(8,128)(2,1)} %copy.108, f32[2,12,72]{2,1,0:T(8,128)S(1)} %get-tuple-element.15, f32[2,12,72,144]{3,2,1,0:T(8,128)} %copy-done.3), kind=kOutput, calls=%fused_computation.39 | convolution fusion | flops 32709456 | bytes 1665792 | tf_op jit(solution)/shard_map/whqk,whke->whqe/dot_general | solution.py:92
  227.9 5.5 %collective-permute-start.6 = (bf16[2,24,3,768]{3,1,2,0:T(8,128)(2,1)}, bf16[2,24,3,768]{3,1,2,0:T(8,128)(2,1)}, u32[]{:S(2)}, u32[]{:S(2)}) collective-permute-start(bf16[2,24,3,768]{3,1,2,0:T(8,128)(2,1)} %param.29), channel_id=1, source_target_pairs={{0,15},{1,0},{2,1},{3,2},{4,3},{5,4},{6,5},{7,6},{8,7},{9,8},{10,9... | collective-permute-start | bytes 663560 | tf_op jit(solution)/shard_map/ppermute | solution.py:20
  258.9 3.6 collective-permute-start.3
  263.2 24.1 %copy.123 = f32[2,12,2,12,3,2,12,6]{1,0,7,6,5,4,3,2:T(2,128)} copy(f32[2,12,2,12,3,2,12,6]{6,5,3,2,1,0,7,4:T(2,128)} %get-tuple-element.13) | data formatting | bytes 1990656 | tf_op jit(solution)/shard_map/vmap()/transpose | solution.py:50
  287.3 15.4 %copy.124 = f32[2,12,72,144]{3,2,1,0:T(8,128)} copy(f32[2,12,72,144]{1,0,3,2:T(2,128)} %bitcast.153) | data formatting | bytes 1990656 | tf_op jit(solution)/shard_map/reshape;vmap()/reshape | solution.py:151
  346.6 3.5 copy.126
  353.1 6.1 %convolution_convert_fusion.3 = bf16[2,12,144,64]{2,3,1,0:T(8,128)(2,1)} fusion(bf16[2,12,72,64]{2,3,1,0:T(8,128)(2,1)} %copy.131, f32[2,12,72]{2,1,0:T(8,128)} %get-tuple-element.17, f32[2,12,72,144]{3,2,1,0:T(8,128)} %copy-done.4), kind=kOutput, calls=%fused_computation.37 | convolution fusion | flops 32820048 | bytes 1665792 | tf_op jit(solution)/shard_map/whqk,whqe->whke/dot_general | solution.py:105
  359.2 13.6 %fusion.31 = bf16[2,12,144,64]{2,3,1,0:T(8,128)(2,1)} fusion(bf16[2,12,72,64]{2,3,1,0:T(8,128)(2,1)} %copy.119, f32[2,12,72,144]{3,2,1,0:T(8,128)} %fusion.98, f32[2,12,72,144]{3,2,1,0:T(8,128)} %get-tuple-element.18, f32[2,12,72]{2,1,0:T(8,128)} %get-tuple-element.17), kind=kOutput, calls=%fused_computation.35 | convolution fusion | flops 33815376 | bytes 2661120 | tf_op jit(solution)/shard_map/whqk,whqe->whke/dot_general | solution.py:104
  379.1 4.4 maximum_bitcast_fusion
  385.7 4.3 reshape.215
  392.0 13.5 %fusion.37 = bf16[2,12,72,64]{2,3,1,0:T(8,128)(2,1)} fusion(bf16[2,12,144,64]{2,3,1,0:T(8,128)(2,1)} %copy.120, f32[2,12,72,144]{3,2,1,0:T(8,128)} %fusion.98, f32[2,12,72,144]{3,2,1,0:T(8,128)} %get-tuple-element.18, f32[2,12,72]{2,1,0:T(8,128)} %get-tuple-element.17), kind=kOutput, calls=%fused_computation.41 | convolution fusion | flops 33704784 | bytes 2661120 | tf_op jit(solution)/shard_map/whqk,whke->whqe/dot_general | solution.py:103
  419.3 6.1 %convolution_convert_fusion.4 = bf16[2,12,72,64]{2,3,1,0:T(8,128)(2,1)} fusion(bf16[2,12,144,64]{2,3,1,0:T(8,128)(2,1)} %copy.126, f32[2,12,72]{2,1,0:T(8,128)} %get-tuple-element.17, f32[2,12,72,144]{3,2,1,0:T(8,128)} %copy-done.4), kind=kOutput, calls=%fused_computation.38 | convolution fusion | flops 32709456 | bytes 1665792 | tf_op jit(solution)/shard_map/whqk,whke->whqe/dot_general | solution.py:92
  455.2 6.2 %convolution_convert_fusion.2 = bf16[2,12,144,64]{2,3,1,0:T(8,128)(2,1)} fusion(bf16[2,12,72,64]{2,3,1,0:T(8,128)(2,1)} %copy.143, f32[2,12,72]{2,1,0:T(8,128)S(1)} %copy-done.21, f32[2,12,72,144]{3,2,1,0:T(8,128)} %copy-done.3), kind=kOutput, calls=%fused_computation.36 | convolution fusion | flops 32820048 | bytes 1665792 | tf_op jit(solution)/shard_map/whqk,whqe->whke/dot_general | solution.py:105
  461.4 13.7 %fusion.28 = bf16[2,12,144,64]{2,3,1,0:T(8,128)(2,1)} fusion(bf16[2,12,72,64]{2,3,1,0:T(8,128)(2,1)} %copy.101, f32[2,12,72,144]{3,2,1,0:T(8,128)} %fusion.99, f32[2,12,72,144]{3,2,1,0:T(8,128)} %get-tuple-element.16, f32[2,12,72]{2,1,0:T(8,128)S(1)} %copy-done.21), kind=kOutput, calls=%fused_computation.34 | convolution fusion | flops 33815376 | bytes 2661120 | tf_op jit(solution)/shard_map/whqk,whqe->whke/dot_general | solution.py:104
  481.4 4.4 maximum_bitcast_fusion.1
  488.0 4.3 reshape.217
  495.9 13.8 %fusion.34 = bf16[2,12,72,64]{2,3,1,0:T(8,128)(2,1)} fusion(bf16[2,12,144,64]{2,3,1,0:T(8,128)(2,1)} %copy.102, f32[2,12,72,144]{3,2,1,0:T(8,128)} %fusion.99, f32[2,12,72,144]{3,2,1,0:T(8,128)} %get-tuple-element.16, f32[2,12,72]{2,1,0:T(8,128)S(1)} %copy-done.21), kind=kOutput, calls=%fused_computation.40 | convolution fusion | flops 33704784 | bytes 2661120 | tf_op jit(solution)/shard_map/whqk,whke->whqe/dot_general | solution.py:103
  517.3 3.5 fusion.92
  (193 shorter events, 198.5 us)
Async XLA Ops:
  0.6 251.3 %copy-start = (bf16[768,2304]{1,0:T(8,128)(2,1)S(1)}, bf16[768,2304]{1,0:T(8,128)(2,1)}, u32[]{:S(2)}) copy-start(bf16[768,2304]{1,0:T(8,128)(2,1)} %param.26) | copy-start | bytes 10616836
  16.5 163.4 %collective-permute-start = (bf16[2,24,3,1536]{3,1,2,0:T(8,128)(2,1)}, bf16[2,24,3,1536]{3,1,2,0:T(8,128)(2,1)}, u32[]{:S(2)}, u32[]{:S(2)}) collective-permute-start(bf16[2,24,3,1536]{3,1,2,0:T(8,128)(2,1)} %copy.98), channel_id=1, source_target_pairs={{0,1},{1,0},{2,3},{3,2},{4,5},{5,4},{6,7},{7,6},{8,9},{9,8},{10,11... | collective-permute-start | bytes 1327112 | tf_op jit(solution)/shard_map/ppermute | solution.py:24
  194.8 1.8 copy-start.3
  194.8 2.1 copy-start.8
  196.6 16.1 %copy-start.20 = (f32[2,12,72]{2,1,0:T(8,128)}, f32[2,12,72]{2,1,0:T(8,128)S(1)}, u32[]{:S(2)}) copy-start(f32[2,12,72]{2,1,0:T(8,128)S(1)} %get-tuple-element.15) | copy-start | bytes 20740
  227.3 6.6 %collective-permute-start.1 = (bf16[2,24,3,768]{3,1,2,0:T(8,128)(2,1)}, bf16[2,24,3,768]{3,1,2,0:T(8,128)(2,1)}, u32[]{:S(2)}, u32[]{:S(2)}) collective-permute-start(bf16[2,24,3,768]{3,1,2,0:T(8,128)(2,1)} %fusion.46), channel_id=1, source_target_pairs={{0,15},{1,0},{2,1},{3,2},{4,3},{5,4},{6,5},{7,6},{8,7},{9,8},{10,9... | collective-permute-start | bytes 663560 | tf_op jit(solution)/shard_map/ppermute | solution.py:20
  227.9 10.8 %collective-permute-start.6 = (bf16[2,24,3,768]{3,1,2,0:T(8,128)(2,1)}, bf16[2,24,3,768]{3,1,2,0:T(8,128)(2,1)}, u32[]{:S(2)}, u32[]{:S(2)}) collective-permute-start(bf16[2,24,3,768]{3,1,2,0:T(8,128)(2,1)} %param.29), channel_id=1, source_target_pairs={{0,15},{1,0},{2,1},{3,2},{4,3},{5,4},{6,5},{7,6},{8,7},{9,8},{10,9... | collective-permute-start | bytes 663560 | tf_op jit(solution)/shard_map/ppermute | solution.py:20
  235.5 5.8 %collective-permute-start.2 = (bf16[2,6,3,768]{3,1,2,0:T(8,128)(2,1)}, bf16[2,6,3,768]{3,1,2,0:T(8,128)(2,1)}, u32[]{:S(2)}, u32[]{:S(2)}) collective-permute-start(bf16[2,6,3,768]{3,1,2,0:T(8,128)(2,1)} %slice.93), channel_id=1, source_target_pairs={{0,16},{16,0},{1,17},{17,1},{2,18},{18,2},{3,19},{19,3},{4,20},{20... | collective-permute-start | bytes 165896 | tf_op jit(solution)/shard_map/ppermute | solution.py:20
  240.2 63.5 %collective-permute-start.7 = (bf16[2,6,3,768]{3,1,2,0:T(8,128)(2,1)}, bf16[2,6,3,768]{3,1,2,0:T(8,128)(2,1)}, u32[]{:S(2)}, u32[]{:S(2)}) collective-permute-start(bf16[2,6,3,768]{3,1,2,0:T(8,128)(2,1)} %slice.101), channel_id=1, source_target_pairs={{0,16},{16,0},{1,17},{17,1},{2,18},{18,2},{3,19},{19,3},{4,20},{20... | collective-permute-start | bytes 165896 | tf_op jit(solution)/shard_map/ppermute | solution.py:20
  241.2 10.8 %copy-start.22 = (f32[768]{0:T(1024)S(1)}, f32[768]{0:T(1024)}, u32[]{:S(2)}) copy-start(f32[768]{0:T(1024)} %param.25) | copy-start | bytes 9220
  254.6 7.9 %copy-start.24 = (pred[2,144]{1,0:T(4,128)(4,1)S(1)}, pred[2,144]{1,0:T(4,128)(4,1)}, u32[]{:S(2)}) copy-start(pred[2,144]{1,0:T(4,128)(4,1)} %eq.52) | copy-start | bytes 868
  256.7 5.7 %copy-start.25 = (pred[2,72]{1,0:T(4,128)(4,1)S(1)}, pred[2,72]{1,0:T(4,128)(4,1)}, u32[]{:S(2)}) copy-start(pred[2,72]{1,0:T(4,128)(4,1)} %eq.50) | copy-start | bytes 436
  258.9 68.9 %collective-permute-start.3 = (bf16[2,24,3,1536]{3,1,2,0:T(8,128)(2,1)}, bf16[2,24,3,1536]{3,1,2,0:T(8,128)(2,1)}, u32[]{:S(2)}, u32[]{:S(2)}) collective-permute-start(bf16[2,24,3,1536]{3,1,2,0:T(8,128)(2,1)} %copy.116), channel_id=1, source_target_pairs={{0,1},{1,0},{2,3},{3,2},{4,5},{5,4},{6,7},{7,6},{8,9},{9,8},{10,11... | collective-permute-start | bytes 1327112 | tf_op jit(solution)/shard_map/ppermute | solution.py:24
  342.6 2.2 copy-start.4
  342.6 2.2 copy-start.7
  392.0 19.7 %collective-permute-start.8 = (bf16[2,24,3,1536]{3,1,2,0:T(8,128)(2,1)}, bf16[2,24,3,1536]{3,1,2,0:T(8,128)(2,1)}, u32[]{:S(2)}, u32[]{:S(2)}) collective-permute-start(bf16[2,24,3,1536]{3,1,2,0:T(8,128)(2,1)} %broadcast_select_fusion.1), channel_id=1, source_target_pairs={{0,1},{1,0},{2,3},{3,2},{4,5},{5,4},{6,7},{7,6},{8,9},{9,8},{10,11... | collective-permute-start | bytes 1327112 | tf_op jit(solution)/shard_map/ppermute | solution.py:24
  411.7 1.5 copy-start.2
  411.7 1.5 copy-start.15
  413.2 2.4 copy-start.10
  418.1 13.5 %collective-permute-start.9 = (bf16[2,6,3,768]{3,1,2,0:T(8,128)(2,1)}, bf16[2,6,3,768]{3,1,2,0:T(8,128)(2,1)}, u32[]{:S(2)}, u32[]{:S(2)}) collective-permute-start(bf16[2,6,3,768]{3,1,2,0:T(8,128)(2,1)} %slice.104), channel_id=1, source_target_pairs={{0,16},{16,0},{1,17},{17,1},{2,18},{18,2},{3,19},{19,3},{4,20},{20... | collective-permute-start | bytes 165896 | tf_op jit(solution)/shard_map/ppermute | solution.py:20
  432.6 7.2 %collective-permute-start.10 = (bf16[2,24,3,768]{3,1,2,0:T(8,128)(2,1)S(1)}, bf16[2,24,3,768]{3,1,2,0:T(8,128)(2,1)S(1)}, u32[]{:S(2)}, u32[]{:S(2)}) collective-permute-start(bf16[2,24,3,768]{3,1,2,0:T(8,128)(2,1)S(1)} %pad_maximum_fusion.3), channel_id=1, source_target_pairs={{0,1},{1,2},{2,3},{3,4},{4,5},{5,6},{6,7},{7,8},{8,9},{9,10},{10,1... | collective-permute-start | bytes 663560 | tf_op jit(solution)/shard_map/ppermute | solution.py:20
  434.5 3.3 collective-permute-start.4
  438.5 57.4 %collective-permute-start.5 = (bf16[2,24,3,768]{3,1,2,0:T(8,128)(2,1)}, bf16[2,24,3,768]{3,1,2,0:T(8,128)(2,1)}, u32[]{:S(2)}, u32[]{:S(2)}) collective-permute-start(bf16[2,24,3,768]{3,1,2,0:T(8,128)(2,1)} %pad_maximum_fusion.1), channel_id=1, source_target_pairs={{0,1},{1,2},{2,3},{3,4},{4,5},{5,6},{6,7},{7,8},{8,9},{9,10},{10,1... | collective-permute-start | bytes 663560 | tf_op jit(solution)/shard_map/ppermute | solution.py:20
  439.9 0.7 copy-start.12
  450.4 4.8 copy-start.21
  494.2 21.5 %collective-permute-start.11 = (bf16[2,24,3,1536]{3,1,2,0:T(8,128)(2,1)}, bf16[2,24,3,1536]{3,1,2,0:T(8,128)(2,1)}, u32[]{:S(2)}, u32[]{:S(2)}) collective-permute-start(bf16[2,24,3,1536]{3,1,2,0:T(8,128)(2,1)} %broadcast_select_fusion), channel_id=1, source_target_pairs={{0,1},{1,0},{2,3},{3,2},{4,5},{5,4},{6,7},{7,6},{8,9},{9,8},{10,11... | collective-permute-start | bytes 1327112 | tf_op jit(solution)/shard_map/ppermute | solution.py:24
  511.6 5.6 %copy-start.17 = (f32[2,24,3]{1,2,0:T(4,128)S(1)}, f32[2,24,3]{1,2,0:T(4,128)}, u32[]{:S(2)}) copy-start(f32[2,24,3]{1,2,0:T(4,128)} %copy-done.16) | copy-start | bytes 1732
  511.6 5.6 %copy-start.19 = (f32[2,24,3]{1,2,0:T(4,128)S(1)}, f32[2,24,3]{1,2,0:T(4,128)}, u32[]{:S(2)}) copy-start(f32[2,24,3]{1,2,0:T(4,128)} %copy-done.18) | copy-start | bytes 1732
  511.6 5.6 %copy-start.23 = (f32[768]{0:T(1024)S(1)}, f32[768]{0:T(1024)}, u32[]{:S(2)}) copy-start(f32[768]{0:T(1024)} %param.21) | copy-start | bytes 9220
  515.8 1.5 copy-start.6
  515.8 1.5 copy-start.14
  517.3 3.5 copy-start.13
  (6 other events, 4.0 us)
where the time goes:
time: 532 us; the launch traced here: 524 us
  local copies, waits for them, and re-layouts  338 us (64%)
  matrix products  112 us (21%)
  other arithmetic  52.6 us (10%)
  starting transfers between devices  16.1 us (3%)
    gather x4, local copies, waits for them, and re-layouts, window_bias_part(): picked = jnp.take(shaped, offset, axis=5)  55.5 us
    transpose x2, local copies, waits for them, and re-layouts, window_bias_part(): picked = picked.transpose(0, 1, 3, 5, 2, 4, 6)  48.3 us
    reshape x4, local copies, waits for them, and re-layouts, window_bias_part(): table.astype(jnp.float32).reshape(heads, WZ, WZ, WLAT, WLAT, 2 * WLON - 1)  41.3 us
    reshape x2, local copies, waits for them, and re-layouts, block_forward(): bias = bias.reshape(windows, heads, -1, bias.shape[-1])  30.8 us
    dot_general x2, matrix products, attend_back(): jnp.einsum('whqk,whqe->whke', grad_scores, queries, preferred_element_typ...  27.3 us
    dot_general x2, matrix products, attend_back(): jnp.einsum('whqk,whke->whqe', grad_scores, keys, preferred_element_type=j...  27.3 us
    squeeze x2, local copies, waits for them, and re-layouts, block_forward(): values = key_values[1]  17.4 us
    transpose x1, other arithmetic, window_bias_part(): picked = picked.transpose(0, 1, 3, 5, 2, 4, 6)  14.2 us
  transfers between devices with their start and end apart: 12, of which 2 were waited for; matrix products, arithmetic and copies ran while one was open for 68% of the time, Pallas kernels for 0%

commit v1 on v0

v1 whole, which is shorter than its diff:
```python
import functools

import jax
import jax.numpy as jnp
import ml_dtypes
import numpy as np
from jax import lax
from jax.experimental import pallas as pl
from jax.experimental.pallas import tpu as pltpu
from jax.sharding import PartitionSpec as P

WZ = 2
WLAT = 12
WLON = 6
LAND = 16
HALF = WLAT // 2
WIDTH = WLON // 2
WINDOWS = 2
TOKENS = WZ * WLAT * WIDTH
SLOT = 80
ROWS = WINDOWS * SLOT
MAIN = 112
STEP = 2 * WLON - 1
RUN = WLAT * STEP
EPS = 1e-05
F32 = jnp.float32
BF16 = jnp.bfloat16
MESH = pl.DeviceIdType.MESH


def window_place(z, r, w):
    return (r // WLAT) * SLOT + w * WZ * WLAT + z * WLAT + r % WLAT


def plain_place(z, r, w):
    return (z * WINDOWS * WLAT + r) * WIDTH + w


def chunk_place(z, r, w, strip):
    chunk = r // HALF
    inner = (z * HALF + r % HALF) * WIDTH + w
    if chunk == strip:
        return MAIN + inner
    return (chunk if strip else chunk - 1) * WZ * HALF * WIDTH + inner


def permutations():
    out = np.zeros((8, ROWS, ROWS), np.float32)
    rows = WINDOWS * WLAT
    for z in range(WZ):
        for r in range(rows):
            for w in range(WIDTH):
                here = window_place(z, r, w)
                plain = plain_place(z, r, w)
                up = chunk_place(z, r, w, 0)
                down = chunk_place(z, r, w, 3)
                from_up = chunk_place(z, (r + HALF) % rows, w, 0)
                from_down = chunk_place(z, (r - HALF) % rows, w, 3)
                out[0, here, plain] = 1
                out[1, up, plain] = 1
                out[2, up, here] = 1
                out[3, here, from_up] = 1
                out[4, down, here] = 1
                out[5, here, from_down] = 1
                out[6, plain, from_down] = 1
                out[7, plain, here] = 1
    return out.astype(ml_dtypes.bfloat16)


def pickers():
    out = np.zeros((2, WZ * 256, WIDTH * 256), np.float32)
    for p in range(2):
        for w in range(WIDTH):
            for slot in range(2):
                for kw in range(WIDTH):
                    col = WIDTH * (p if slot == 0 else 1 - p) + kw
                    d = WIDTH * p + w - col + WLON - 1
                    for z in range(WZ):
                        for r in range(WLAT):
                            key = slot * SLOT + kw * WZ * WLAT + z * WLAT + r
                            out[p, z * 256 + r * STEP + d, w * 256 + key] = 1
    return out.astype(ml_dtypes.bfloat16)


def key_rows():
    out = np.zeros((8, 256), np.float32)
    for slot in range(2):
        for k in range(SLOT):
            upper = k % WLAT >= HALF
            lane = slot * SLOT + k
            if k >= TOKENS:
                out[0, lane] = -1e30
            else:
                out[1, lane] = -1e9 if upper else 0.0
                out[2, lane] = 0.0 if upper else -1e9
    return out


def land_pickers():
    rows = np.zeros((ROWS, WINDOWS * WLAT), np.float32)
    cols = np.zeros((ROWS, WIDTH), np.float32)
    for z in range(WZ):
        for r in range(WINDOWS * WLAT):
            for w in range(WIDTH):
                here = window_place(z, r, w)
                rows[here, r] = 1
                cols[here, w] = 1
    return rows.astype(ml_dtypes.bfloat16), cols


def mm(a, b):
    return lax.dot_general(a, b, (((1,), (0,)), ((), ())), preferred_element_type=F32)


def mt(a, b):
    return lax.dot_general(a, b, (((1,), (1,)), ((), ())), preferred_element_type=F32)


def tm(a, b):
    return lax.dot_general(a, b, (((0,), (0,)), ((), ())), preferred_element_type=F32)


def kernel(
    lats,
    lons,
    stream,
    land,
    orography,
    land_vector,
    orography_table,
    gain_one,
    qkv_one,
    proj_one,
    gain_two,
    qkv_two,
    proj_two,
    tables,
    cotangent,
    perms,
    picks,
    keys_row,
    land_rows,
    land_cols,
    output,
    grad_stream,
    bias,
    spread,
    probs,
    field,
    normed,
    inverse,
    qkv,
    far,
    mixed,
    back,
    grads,
    far_grads,
    got_grads,
    sent,
    got,
    send_sem,
    recv_sem,
):
    dims = stream.shape[1]
    heads = tables.shape[1] // WINDOWS
    pairs = heads // 2
    i = lax.axis_index("lat")
    j = lax.axis_index("lon")
    parity = lax.rem(j, 2)
    next_lat = lax.rem(i + 1, lats)
    prev_lat = lax.rem(i + lats - 1, lats)
    east = lax.rem(j + 1, lons)
    west = lax.rem(j + lons - 1, lons)
    partner = (i, j + 1 - 2 * parity)

    barrier = pltpu.get_barrier_semaphore()
    for peer in ((i, east), (i, west), (next_lat, east), (prev_lat, west)):
        pl.semaphore_signal(barrier, inc=1, device_id=peer, device_id_type=MESH)

    copies = []

    def send(src, dst, to):
        n = len(copies)
        copy = pltpu.make_async_remote_copy(
            src_ref=src,
            dst_ref=dst,
            send_sem=send_sem.at[n],
            recv_sem=recv_sem.at[n],
            device_id=to,
            device_id_type=MESH,
        )
        copy.start()
        copies.append(copy)
        return copy

    def roll(slot, moved, up):
        sent[slot] = moved.astype(BF16)
        main = (i, west) if up else (i, east)
        strip = (prev_lat, west) if up else (next_lat, east)
        a = send(sent.at[slot, pl.ds(0, MAIN)], got.at[slot, pl.ds(0, MAIN)], main)
        rest = pl.ds(MAIN, ROWS - MAIN)
        b = send(sent.at[slot, rest], got.at[slot, rest], strip)
        return a, b

    def arrive(both):
        for copy in both:
            copy.wait_recv()

    plain = WZ * WINDOWS * WLAT * WIDTH

    row_pick = land_rows[...]
    col_pick = land_cols[...]

    def per_token(ref):
        spread_rows = mm(row_pick, ref[...].astype(F32).astype(BF16))
        return jnp.sum(spread_rows * col_pick, axis=1, keepdims=True)

    classes = per_token(orography)
    added = (per_token(land) * (1.0 / LAND)) * land_vector[...]
    for k in range(orography_table.shape[0]):
        added = added + jnp.where(classes == float(k), 1.0, 0.0) * orography_table[k : k + 1, :]
    embedded = (mm(perms[0, :, :plain], stream[...]) + added).astype(BF16)
    field[0] = embedded

    def project(b, gain, weight):
        values = field[b].astype(F32)
        centred = values - jnp.mean(values, axis=-1, keepdims=True)
        inv = lax.rsqrt(jnp.mean(centred * centred, axis=-1, keepdims=True) + EPS)
        norm = centred * inv
        normed[b] = norm
        inverse[b] = inv
        h = (norm * gain[...]).astype(BF16)
        for part in (1, 2, 0):
            cols = slice(part * dims, (part + 1) * dims)
            qkv[b, :, cols] = mm(h, weight[:, cols]).astype(BF16)

    project(0, gain_one, qkv_one)
    pl.semaphore_wait(barrier, 4)
    kv_one = send(qkv.at[0, :, pl.ds(dims, 2 * dims)], far.at[0], partner)
    cot = roll(0, mm(perms[1, :, :plain], cotangent[...]), True)

    pick = picks[parity]
    last = jnp.where(i == lats - 1, 1.0, 0.0).astype(F32)
    pad_row = keys_row[0:1, :]
    count = WINDOWS * heads
    late = lax.broadcasted_iota(jnp.int32, (count, 256), 0) >= heads

    def expand(b):
        entries = tables[b].astype(F32)
        for za in range(WZ):
            for ra in range(WLAT):
                n = za * WLAT + ra
                for zc in range(WZ):
                    k = (za * WZ + zc) * WLAT + ra
                    spread[n * count : (n + 1) * count, zc * 256 : (zc + 1) * 256] = entries[
                        :, RUN * k : RUN * k + 256
                    ]
        for tn in range(count):
            bias[b, :, tn * SLOT + TOKENS : (tn + 1) * SLOT, :] = jnp.zeros(
                (2, SLOT - TOKENS, 128), F32
            )
        group = 4
        for first in range(0, WZ * WLAT, group):
            rows = spread[first * count : (first + group) * count, :].astype(BF16)
            for w in range(WIDTH):
                picked = mm(rows, pick[:, w * 256 : (w + 1) * 256])
                for g in range(group):
                    n = first + g
                    value = picked[g * count : (g + 1) * count, :] + pad_row
                    if b == 1:
                        forbid = keys_row[1:2, :] if n % WLAT < HALF else keys_row[2:3, :]
                        value = value + jnp.where(late, last * forbid, 0.0)
                    for half in range(2):
                        bias[b, half, pl.ds(w * WZ * WLAT + n, count, stride=SLOT), :] = value[
                            :, half * 128 : (half + 1) * 128
                        ]

    expand(0)

    low = lax.broadcasted_iota(jnp.int32, (SLOT, 128), 1) < 64
    first_half = jnp.where(low, 1.0, 0.0).astype(BF16)
    second_half = jnp.where(low, 0.0, 1.0).astype(BF16)
    scale = (dims // heads) ** -0.5

    def split(value):
        return jnp.concatenate([value * first_half, value * second_half], axis=0)

    def merge(value):
        return jnp.where(low, value[:SLOT], value[SLOT:])

    def lanes(part, pair):
        return pl.ds(pl.multiple_of(part * dims + pair * 128, 128), 128)

    def keys_of(b, rows, part, pair):
        own = qkv[b, rows, lanes(part + 1, pair)]
        other = far[b, rows, lanes(part, pair)]
        return jnp.concatenate([own, other], axis=0)

    def forward(b, t, pair, rows):
        q = split(qkv[b, rows, lanes(0, pair)])
        k = keys_of(b, rows, 0, pair)
        v = keys_of(b, rows, 1, pair)
        at = pl.multiple_of((t * heads + 2 * pair) * SLOT, SLOT)
        here = pl.ds(at, 2 * SLOT)
        offsets = jnp.concatenate([bias[b, 0, here, :], bias[b, 1, here, : 2 * SLOT - 128]], axis=1)
        scores = mt(q, k) * scale + offsets
        expo = jnp.exp(scores - jnp.max(scores, axis=-1, keepdims=True))
        p = expo * (1.0 / jnp.sum(expo, axis=-1, keepdims=True))
        rounded = p.astype(BF16)
        mixed[rows, lanes(0, pair)] = merge(mm(rounded, v)).astype(BF16)
        return q, k, v, p, rounded

    def backward(rows, pair, q, k, v, p, rounded):
        d = split(back[rows, lanes(0, pair)])
        dp = mt(d, v)
        inner = jnp.sum(p * dp, axis=-1, keepdims=True)
        ds = (p * (dp - inner) * scale).astype(BF16)
        grads[rows, lanes(0, pair)] = merge(mm(ds, k)).astype(BF16)
        dk = tm(ds, q).astype(BF16)
        dv = tm(rounded, d).astype(BF16)
        grads[rows, lanes(1, pair)] = dk[:SLOT]
        grads[rows, lanes(2, pair)] = dv[:SLOT]
        far_grads[rows, lanes(0, pair)] = dk[SLOT:]
        far_grads[rows, lanes(1, pair)] = dv[SLOT:]

    def save_at(t, pair):
        return pl.ds(pl.multiple_of((t * heads + 2 * pair) * SLOT, SLOT), 2 * SLOT)

    def finish(b, dy, gain, weight):
        dq = grads[:, :dims]
        total = mt(dq, weight[:, :dims])
        for part in (1, 2):
            cols = slice(part * dims, (part + 1) * dims)
            own = grads[:, cols].astype(F32)
            other = got_grads[b, :, (part - 1) * dims : part * dims].astype(F32)
            total = total + mt((own + other).astype(BF16), weight[:, cols])
        scaled = total * gain[...]
        norm = normed[b]
        mean = jnp.mean(scaled, axis=-1, keepdims=True)
        along = jnp.mean(scaled * norm, axis=-1, keepdims=True)
        return (dy + (scaled - mean - norm * along) * inverse[b]).astype(BF16)

    kv_one.wait_recv()

    def one(pair, carry):
        for t in range(WINDOWS):
            rows = pl.ds(t * SLOT, SLOT)
            saved = forward(0, t, pair, rows)
            probs[save_at(t, pair), :] = saved[3]
        return carry

    lax.fori_loop(0, pairs, one, 0)
    middle = (field[0].astype(F32) + mm(mixed[...], proj_one[...])).astype(BF16)
    moved = roll(1, mm(perms[2], middle), True)
    expand(1)
    arrive(moved)
    field[1] = mm(perms[3], got[1]).astype(BF16)

    project(1, gain_two, qkv_two)
    kv_two = send(qkv.at[1, :, pl.ds(dims, 2 * dims)], far.at[1], partner)
    arrive(cot)
    dy_two = mm(perms[3], got[0])
    back[...] = mt(dy_two.astype(BF16), proj_two[...]).astype(BF16)
    kv_two.wait_recv()

    def two(pair, carry):
        for t in range(WINDOWS):
            rows = pl.ds(t * SLOT, SLOT)
            backward(rows, pair, *forward(1, t, pair, rows))
        return carry

    lax.fori_loop(0, pairs, two, 0)
    dkv_two = send(far_grads, got_grads.at[1], partner)
    turned = (field[1].astype(F32) + mm(mixed[...], proj_two[...])).astype(BF16)
    result = roll(2, mm(perms[4], turned), False)
    dkv_two.wait_recv()
    grad_turned = finish(1, mm(perms[3], got[0]), gain_two, qkv_two)
    moved = roll(3, mm(perms[4], grad_turned), False)
    arrive(result)
    output[...] = mm(perms[6], got[2])[:plain].astype(BF16)
    arrive(moved)

    dy_one = mm(perms[5], got[3])
    back[...] = mt(dy_one.astype(BF16), proj_one[...]).astype(BF16)
    dkv_two.wait_send()

    def one_back(pair, carry):
        for t in range(WINDOWS):
            rows = pl.ds(t * SLOT, SLOT)
            q = split(qkv[0, rows, lanes(0, pair)])
            p = probs[save_at(t, pair), :]
            k = keys_of(0, rows, 0, pair)
            v = keys_of(0, rows, 1, pair)
            backward(rows, pair, q, k, v, p, p.astype(BF16))
        return carry

    lax.fori_loop(0, pairs, one_back, 0)
    dkv_one = send(far_grads, got_grads.at[0], partner)
    dkv_one.wait_recv()
    last_grad = finish(0, mm(perms[5], got[3]), gain_one, qkv_one)
    grad_stream[...] = mm(perms[7], last_grad)[:plain].astype(BF16)
    for copy in copies:
        if copy is not dkv_two:
            copy.wait_send()


def body(
    lats,
    lons,
    stream,
    land,
    orography,
    land_vector,
    orography_table,
    gain_one,
    qkv_one,
    proj_one,
    table_one,
    gain_two,
    qkv_two,
    proj_two,
    table_two,
    cotangent,
):
    levels, rows, width, dims = stream.shape
    types, heads, entries = table_one.shape
    plain = levels * rows * width
    tables = jnp.stack([table_one, table_two]).reshape(2, types * heads, entries)
    tables = jnp.pad(tables, ((0, 0), (0, 0), (0, 128)))
    land_rows, land_cols = land_pickers()
    wide = 3 * dims
    scratch = [
        pltpu.VMEM((2, 2, types * heads * SLOT, 128), F32),
        pltpu.VMEM((WZ * WLAT * types * heads, WZ * 256), F32),
        pltpu.VMEM((types * heads * SLOT, 2 * SLOT), F32),
        pltpu.VMEM((2, ROWS, dims), BF16),
        pltpu.VMEM((2, ROWS, dims), F32),
        pltpu.VMEM((2, ROWS, 1), F32),
        pltpu.VMEM((2, ROWS, wide), BF16),
        pltpu.VMEM((2, ROWS, 2 * dims), BF16),
        pltpu.VMEM((ROWS, dims), BF16),
        pltpu.VMEM((ROWS, dims), BF16),
        pltpu.VMEM((ROWS, wide), BF16),
        pltpu.VMEM((ROWS, 2 * dims), BF16),
        pltpu.VMEM((2, ROWS, 2 * dims), BF16),
        pltpu.VMEM((4, ROWS, dims), BF16),
        pltpu.VMEM((4, ROWS, dims), BF16),
        pltpu.SemaphoreType.DMA((12,)),
        pltpu.SemaphoreType.DMA((12,)),
    ]
    vmem = pl.BlockSpec(memory_space=pltpu.VMEM)
    out, grad = pl.pallas_call(
        functools.partial(kernel, lats, lons),
        out_shape=[jax.ShapeDtypeStruct((plain, dims), BF16)] * 2,
        in_specs=[vmem] * 18,
        out_specs=[vmem] * 2,
        scratch_shapes=scratch,
        compiler_params=pltpu.CompilerParams(
            collective_id=0, has_side_effects=True, vmem_limit_bytes=56 << 20
        ),
    )(
        stream.reshape(plain, dims),
        land,
        orography,
        land_vector.reshape(1, dims),
        orography_table,
        gain_one.reshape(1, dims),
        qkv_one,
        proj_one,
        gain_two.reshape(1, dims),
        qkv_two,
        proj_two,
        tables,
        cotangent.reshape(plain, dims),
        jnp.asarray(permutations()),
        jnp.asarray(pickers()),
        jnp.asarray(key_rows()),
        jnp.asarray(land_rows),
        jnp.asarray(land_cols),
    )
    return out.reshape(stream.shape), grad.reshape(stream.shape)


def solution(mesh):
    placed = (
        P(None, "lat", "lon", None),
        P("lat", "lon"),
        P("lat", "lon"),
        P(),
        P(),
        P(),
        P(),
        P(),
        P("lat", None, None),
        P(),
        P(),
        P(),
        P("lat", None, None),
        P(None, "lat", "lon", None),
    )
    return jax.shard_map(
        functools.partial(body, mesh.shape["lat"], mesh.shape["lon"]),
        mesh=mesh,
        in_specs=placed,
        out_specs=(P(None, "lat", "lon", None), P(None, "lat", "lon", None)),
        check_vma=False,
    )
```

time: 532 us -> 67.6 us (0.13); the launches traced: 524 us -> 67.4 us
  local copies, waits for them, and re-layouts: 338 us -> 10 us
  matrix products: 112 us -> 0 us
  Pallas kernels: 0 us -> 55.7 us
  other arithmetic: 52.6 us -> 0.9 us
  starting transfers between devices: 16.1 us -> 0 us
    dot_general x21 -> x0, matrix products: 112 us -> none  [the longest x2 27.3 us: attend_back(): jnp.einsum('whqk,whqe->whke', grad_scores, queries, preferred_element_typ...]
    reshape x15 -> x7, local copies, waits for them, and re-layouts: 94.8 us -> 5.61 us  [the longest x2 2.09 us: body(): return (out.reshape(stream.shape), grad.reshape(stream.shape))]
    transpose x10 -> x0, local copies, waits for them, and re-layouts: 65.8 us -> none  [the longest x2 48.3 us: window_bias_part(): picked = picked.transpose(0, 1, 3, 5, 2, 4, 6)]
    pallas_call x0 -> x1, Pallas kernels: none -> 55.7 us  [body(): pl.pallas_call(functools.partial(kernel, lats, lons), out_shape=[jax.Shap...]
    gather x4 -> x0, local copies, waits for them, and re-layouts: 55.5 us -> none  [window_bias_part(): picked = jnp.take(shaped, offset, axis=5)]
    convert_element_type x15 -> x0, local copies, waits for them, and re-layouts: 32.7 us -> none  [the longest x4 12.6 us: attend_back(): return (grad_q, grad_k.astype(jnp.bfloat16), grad_v.astype(jnp.bfloat16))]
    transpose x5 -> x0, other arithmetic: 30 us -> none  [the longest x1 14.2 us: window_bias_part(): picked = picked.transpose(0, 1, 3, 5, 2, 4, 6)]
    slice x20 -> x0, local copies, waits for them, and re-layouts: 25.5 us -> none  [the longest x4 6.62 us: block_forward(): keys = key_values[0]]
  transfers between devices with their start and end apart: 12 -> 0, of which waited for: 2 -> 0; matrix products, arithmetic and copies ran while one was open for 68% -> 0% of each run, Pallas kernels for 0% -> 0%
where the time goes in v1:
time: 67.6 us; the launch traced here: 67.4 us
  Pallas kernels  55.7 us (82%)
  local copies, waits for them, and re-layouts  10 us (15%)
  other arithmetic  0.9 us (1%)
  between operations  0.74 us (1%)
    pallas_call x1, Pallas kernels, body(): pl.pallas_call(functools.partial(kernel, lats, lons), out_shape=[jax.Shap...  55.7 us
    unnamed x24, local copies, waits for them, and re-layouts  4.15 us
    reshape x2, local copies, waits for them, and re-layouts, body(): return (out.reshape(stream.shape), grad.reshape(stream.shape))  2.09 us

profile of v1, /device:TPU:1, one launch (start us, length us, event | category | flops | bytes accessed | tf_op | source)
XLA Modules:
  0.0 67.4 jit_solution(11417813754684606499)
XLA Ops:
  0.6 0.0 copy-start
  0.6 1.1 %copy.31 = bf16[2,12,6336]{2,1,0:T(8,128)(2,1)S(1)} copy(bf16[2,12,6336]{2,0,1:T(2,128)(2,1)} %param.31) | data formatting | bytes 608256 | tf_op args[12]
  1.7 0.1 stack.10
  1.8 0.0 copy-done
  1.8 0.0 copy-start.1
  1.9 0.1 stack.9
  2.0 0.0 copy-start.2
  2.0 0.9 %fusion.2.tables = bf16[2,24,6464]{2,1,0:T(8,128)(2,1)} fusion(bf16[1,24,6336]{2,1,0:T(8,128)(2,1)S(1)} %stack.10, bf16[1,24,6336]{2,1,0:T(8,128)(2,1)S(1)} %stack.9), kind=kLoop, calls=%fused_computation.3 | loop fusion | flops 2171904 | bytes 1228800 | tf_op jit(solution)/shard_map/stack | solution.py:428
  2.9 0.0 copy-done.1
  2.9 0.0 copy-start.6
  3.0 0.0 copy-start.4
  3.0 0.0 copy-start.5
  3.0 0.1 copy.29
  3.1 0.9 %reshape.30.stream = bf16[144,768]{1,0:T(8,128)(2,1)} reshape(bf16[2,24,3,768]{3,2,1,0:T(4,128)(2,1)S(1)} %copy.29) | data formatting | bytes 442368 | tf_op jit(solution)/shard_map/reshape | solution.py:462
  4.0 0.0 copy-done.2
  4.0 0.1 copy.32
  4.1 0.9 %reshape.34.cotangent = bf16[144,768]{1,0:T(8,128)(2,1)} reshape(bf16[2,24,3,768]{3,2,1,0:T(4,128)(2,1)S(1)} %copy.32) | data formatting | bytes 442368 | tf_op jit(solution)/shard_map/reshape | solution.py:474
  5.0 0.0 copy-done.6
  5.0 0.7 %copy.33.land = s32[24,3]{1,0:T(8,128)} copy(s32[24,3]{0,1:T(4,128)S(1)} %copy-done.6) | data formatting | bytes 576 | tf_op args[1]
  5.6 0.0 copy-done.7
  5.7 0.7 %copy.34.orography = s32[24,3]{1,0:T(8,128)} copy(s32[24,3]{0,1:T(4,128)S(1)} %copy-done.7) | data formatting | bytes 576 | tf_op args[2]
  6.3 0.0 copy-done.3
  6.3 0.6 reshape.31.land_vector
  6.9 0.0 copy-done.4
  6.9 0.6 reshape.32.gain_one
  7.5 0.0 copy-done.5
  7.5 0.6 reshape.33.gain_two
  8.1 55.7 %shard_map.194 = (bf16[144,768]{1,0:T(8,128)(2,1)}, bf16[144,768]{1,0:T(8,128)(2,1)}) custom-call(bf16[144,768]{1,0:T(8,128)(2,1)} %reshape.30.stream, s32[24,3]{1,0:T(8,128)} %copy.33.land, s32[24,3]{1,0:T(8,128)} %copy.34.orography, f32[1,768]{1,0:T(1,128)} %reshape.31.land_vector, f32[8,768]{1,0:T(8,128)} %orography_table.1, f32[1,768]{1,0:T(1,128)} %reshape.32.gain_one, ...), custom_call_target="tpu_custom_call" | custom-call | tf_op jit(solution)/shard_map/pallas_call | solution.py:452
  63.9 1.0 %reshape.35 = bf16[2,24,3,768]{3,2,1,0:T(4,128)(2,1)S(1)} reshape(bf16[144,768]{1,0:T(8,128)(2,1)} %get-tuple-element.4) | data formatting | bytes 442368 | tf_op jit(solution)/shard_map/reshape | solution.py:481
  64.9 0.7 %copy.35 = bf16[2,24,3,768]{3,1,2,0:T(8,128)(2,1)} copy(bf16[2,24,3,768]{3,2,1,0:T(4,128)(2,1)S(1)} %reshape.35) | data formatting | bytes 442368
  65.6 1.0 %reshape.36 = bf16[2,24,3,768]{3,2,1,0:T(4,128)(2,1)S(1)} reshape(bf16[144,768]{1,0:T(8,128)(2,1)} %get-tuple-element.5) | data formatting | bytes 442368 | tf_op jit(solution)/shard_map/reshape | solution.py:481
  66.7 0.7 %copy.36 = bf16[2,24,3,768]{3,1,2,0:T(8,128)(2,1)} copy(bf16[2,24,3,768]{3,2,1,0:T(4,128)(2,1)S(1)} %reshape.36) | data formatting | bytes 442368
  (3 shorter events, 0.0 us)
Async XLA Ops:
  0.6 1.2 %copy-start = (bf16[2,12,6336]{2,0,1:T(2,128)(2,1)S(1)}, bf16[2,12,6336]{2,0,1:T(2,128)(2,1)}, u32[]{:S(2)}) copy-start(bf16[2,12,6336]{2,0,1:T(2,128)(2,1)} %param.27) | copy-start | bytes 912388
  1.8 1.1 %copy-start.1 = (bf16[2,24,3,768]{3,1,2,0:T(8,128)(2,1)S(1)}, bf16[2,24,3,768]{3,1,2,0:T(8,128)(2,1)}, u32[]{:S(2)}) copy-start(bf16[2,24,3,768]{3,1,2,0:T(8,128)(2,1)} %param.19) | copy-start | bytes 663556
  2.0 1.9 %copy-start.2 = (bf16[2,24,3,768]{3,1,2,0:T(8,128)(2,1)S(1)}, bf16[2,24,3,768]{3,1,2,0:T(8,128)(2,1)}, u32[]{:S(2)}) copy-start(bf16[2,24,3,768]{3,1,2,0:T(8,128)(2,1)} %param.32) | copy-start | bytes 663556
  2.9 2.0 %copy-start.6 = (s32[24,3]{0,1:T(4,128)S(1)}, s32[24,3]{0,1:T(4,128)}, u32[]{:S(2)}) copy-start(s32[24,3]{0,1:T(4,128)} %param.20) | copy-start | bytes 868
  2.9 2.7 %copy-start.7 = (s32[24,3]{0,1:T(4,128)S(1)}, s32[24,3]{0,1:T(4,128)}, u32[]{:S(2)}) copy-start(s32[24,3]{0,1:T(4,128)} %param.21) | copy-start | bytes 868
  2.9 3.4 %copy-start.3 = (f32[768]{0:T(1024)S(1)}, f32[768]{0:T(1024)}, u32[]{:S(2)}) copy-start(f32[768]{0:T(1024)} %param.22) | copy-start | bytes 9220
  3.0 4.0 %copy-start.4 = (f32[768]{0:T(1024)S(1)}, f32[768]{0:T(1024)}, u32[]{:S(2)}) copy-start(f32[768]{0:T(1024)} %param.24) | copy-start | bytes 9220
  3.0 4.6 %copy-start.5 = (f32[768]{0:T(1024)S(1)}, f32[768]{0:T(1024)}, u32[]{:S(2)}) copy-start(f32[768]{0:T(1024)} %param.28) | copy-start | bytes 9220

commit v2 on v1

--- a/solution.py
+++ b/solution.py
@@ -33,7 +33,7 @@
 
 
 def plain_place(z, r, w):
-    return (z * WINDOWS * WLAT + r) * WIDTH + w
+    return (z * WIDTH + w) * WINDOWS * WLAT + r
 
 
 def chunk_place(z, r, w, strip):
@@ -129,15 +129,16 @@
     land_vector,
     orography_table,
     gain_one,
-    qkv_one,
-    proj_one,
+    hbm_qkv_one,
+    hbm_proj_one,
     gain_two,
-    qkv_two,
-    proj_two,
-    tables,
+    hbm_qkv_two,
+    hbm_proj_two,
+    table_one,
+    table_two,
     cotangent,
     perms,
-    picks,
+    hbm_picks,
     keys_row,
     land_rows,
     land_cols,
@@ -145,6 +146,7 @@
     grad_stream,
     bias,
     spread,
+    entries,
     probs,
     field,
     normed,
@@ -160,9 +162,16 @@
     got,
     send_sem,
     recv_sem,
+    qkv_one,
+    proj_one,
+    qkv_two,
+    proj_two,
+    pick,
+    load_sem,
 ):
     dims = stream.shape[1]
-    heads = tables.shape[1] // WINDOWS
+    heads = table_one.shape[0]
+    tables = (table_one, table_two)
     pairs = heads // 2
     i = lax.axis_index("lat")
     j = lax.axis_index("lon")
@@ -172,6 +181,18 @@
     east = lax.rem(j + 1, lons)
     west = lax.rem(j + lons - 1, lons)
     partner = (i, j + 1 - 2 * parity)
+
+    loads = []
+    for source, target in (
+        (hbm_qkv_one, qkv_one),
+        (hbm_picks.at[parity], pick),
+        (hbm_proj_one, proj_one),
+        (hbm_qkv_two, qkv_two),
+        (hbm_proj_two, proj_two),
+    ):
+        load = pltpu.make_async_copy(source, target, load_sem.at[len(loads)])
+        load.start()
+        loads.append(load)
 
     barrier = pltpu.get_barrier_semaphore()
     for peer in ((i, east), (i, west), (next_lat, east), (prev_lat, west)):
@@ -212,11 +233,11 @@
     col_pick = land_cols[...]
 
     def per_token(ref):
-        spread_rows = mm(row_pick, ref[...].astype(F32).astype(BF16))
+        spread_rows = mt(row_pick, ref[...].astype(F32).astype(BF16))
         return jnp.sum(spread_rows * col_pick, axis=1, keepdims=True)
 
     classes = per_token(orography)
-    added = (per_token(land) * (1.0 / LAND)) * land_vector[...]
+    added = (per_token(land) * (1.0 / LAND)) * land_vector[...].reshape(1, dims)
     for k in range(orography_table.shape[0]):
         added = added + jnp.where(classes == float(k), 1.0, 0.0) * orography_table[k : k + 1, :]
     embedded = (mm(perms[0, :, :plain], stream[...]) + added).astype(BF16)
@@ -229,37 +250,45 @@
         norm = centred * inv
         normed[b] = norm
         inverse[b] = inv
-        h = (norm * gain[...]).astype(BF16)
-        for part in (1, 2, 0):
+        h = (norm * gain[...].reshape(1, dims)).astype(BF16)
+        loads[0 if b == 0 else 3].wait()
+        for part in (1, 2):
             cols = slice(part * dims, (part + 1) * dims)
             qkv[b, :, cols] = mm(h, weight[:, cols]).astype(BF16)
-
-    project(0, gain_one, qkv_one)
-    pl.semaphore_wait(barrier, 4)
-    kv_one = send(qkv.at[0, :, pl.ds(dims, 2 * dims)], far.at[0], partner)
+        if b == 0:
+            pl.semaphore_wait(barrier, 4)
+        copy = send(qkv.at[b, :, pl.ds(dims, 2 * dims)], far.at[b], partner)
+        qkv[b, :, :dims] = mm(h, weight[:, :dims]).astype(BF16)
+        return copy
+
+    kv_one = project(0, gain_one, qkv_one)
     cot = roll(0, mm(perms[1, :, :plain], cotangent[...]), True)
 
-    pick = picks[parity]
+    loads[1].wait()
     last = jnp.where(i == lats - 1, 1.0, 0.0).astype(F32)
     pad_row = keys_row[0:1, :]
     count = WINDOWS * heads
-    late = lax.broadcasted_iota(jnp.int32, (count, 256), 0) >= heads
+    late = lax.broadcasted_iota(jnp.int32, (count, 256), 0) % WINDOWS == WINDOWS - 1
 
     def expand(b):
-        entries = tables[b].astype(F32)
+        for n in range(heads):
+            entries[n * WINDOWS : (n + 1) * WINDOWS, :] = tables[b][n].astype(F32)
         for za in range(WZ):
             for ra in range(WLAT):
                 n = za * WLAT + ra
                 for zc in range(WZ):
                     k = (za * WZ + zc) * WLAT + ra
-                    spread[n * count : (n + 1) * count, zc * 256 : (zc + 1) * 256] = entries[
-                        :, RUN * k : RUN * k + 256
-                    ]
+                    stop = min(RUN * k + 256, entries.shape[1])
+                    run = entries[:, RUN * k : stop]
+                    if run.shape[1] < 256:
+                        rest = jnp.zeros((count, 256 - run.shape[1]), F32)
+                        run = jnp.concatenate([run, rest], axis=1)
+                    spread[n * count : (n + 1) * count, zc * 256 : (zc + 1) * 256] = run
         for tn in range(count):
             bias[b, :, tn * SLOT + TOKENS : (tn + 1) * SLOT, :] = jnp.zeros(
                 (2, SLOT - TOKENS, 128), F32
             )
-        group = 4
+        group = WLAT
         for first in range(0, WZ * WLAT, group):
             rows = spread[first * count : (first + group) * count, :].astype(BF16)
             for w in range(WIDTH):
@@ -300,9 +329,13 @@
         q = split(qkv[b, rows, lanes(0, pair)])
         k = keys_of(b, rows, 0, pair)
         v = keys_of(b, rows, 1, pair)
-        at = pl.multiple_of((t * heads + 2 * pair) * SLOT, SLOT)
-        here = pl.ds(at, 2 * SLOT)
-        offsets = jnp.concatenate([bias[b, 0, here, :], bias[b, 1, here, : 2 * SLOT - 128]], axis=1)
+        at = pl.multiple_of((2 * pair * WINDOWS + t) * SLOT, SLOT)
+        parts = []
+        for start in (at, pl.multiple_of(at + WINDOWS * SLOT, SLOT)):
+            here = pl.ds(start, SLOT)
+            row = [bias[b, 0, here, :], bias[b, 1, here, : 2 * SLOT - 128]]
+            parts.append(jnp.concatenate(row, axis=1))
+        offsets = jnp.concatenate(parts, axis=0)
         scores = mt(q, k) * scale + offsets
         expo = jnp.exp(scores - jnp.max(scores, axis=-1, keepdims=True))
         p = expo * (1.0 / jnp.sum(expo, axis=-1, keepdims=True))
@@ -310,7 +343,7 @@
         mixed[rows, lanes(0, pair)] = merge(mm(rounded, v)).astype(BF16)
         return q, k, v, p, rounded
 
-    def backward(rows, pair, q, k, v, p, rounded):
+    def backward(b, rows, pair, q, k, v, p, rounded):
         d = split(back[rows, lanes(0, pair)])
         dp = mt(d, v)
         inner = jnp.sum(p * dp, axis=-1, keepdims=True)
@@ -320,21 +353,34 @@
         dv = tm(rounded, d).astype(BF16)
         grads[rows, lanes(1, pair)] = dk[:SLOT]
         grads[rows, lanes(2, pair)] = dv[:SLOT]
-        far_grads[rows, lanes(0, pair)] = dk[SLOT:]
-        far_grads[rows, lanes(1, pair)] = dv[SLOT:]
+        far_grads[b, rows, lanes(0, pair)] = dk[SLOT:]
+        far_grads[b, rows, lanes(1, pair)] = dv[SLOT:]
 
     def save_at(t, pair):
         return pl.ds(pl.multiple_of((t * heads + 2 * pair) * SLOT, SLOT), 2 * SLOT)
 
-    def finish(b, dy, gain, weight):
+    def halves(body, b):
+        sends = []
+        cut = pairs // 2
+        for first, last_pair in ((0, cut), (cut, pairs)):
+            lax.fori_loop(first, last_pair, body, 0, unroll=True)
+            for part in range(2):
+                cols = pl.ds(part * dims + first * 128, (last_pair - first) * 128)
+                sends.append(
+                    send(far_grads.at[b, :, cols], got_grads.at[b, :, cols], partner)
+                )
+        return sends
+
+    def finish(b, dy, gain, weight, sends):
         dq = grads[:, :dims]
         total = mt(dq, weight[:, :dims])
+        arrive(sends)
         for part in (1, 2):
             cols = slice(part * dims, (part + 1) * dims)
             own = grads[:, cols].astype(F32)
             other = got_grads[b, :, (part - 1) * dims : part * dims].astype(F32)
             total = total + mt((own + other).astype(BF16), weight[:, cols])
-        scaled = total * gain[...]
+        scaled = total * gain[...].reshape(1, dims)
         norm = normed[b]
         mean = jnp.mean(scaled, axis=-1, keepdims=True)
         along = jnp.mean(scaled * norm, axis=-1, keepdims=True)
@@ -349,15 +395,16 @@
             probs[save_at(t, pair), :] = saved[3]
         return carry
 
-    lax.fori_loop(0, pairs, one, 0)
+    lax.fori_loop(0, pairs, one, 0, unroll=True)
+    loads[2].wait()
     middle = (field[0].astype(F32) + mm(mixed[...], proj_one[...])).astype(BF16)
     moved = roll(1, mm(perms[2], middle), True)
     expand(1)
     arrive(moved)
     field[1] = mm(perms[3], got[1]).astype(BF16)
 
-    project(1, gain_two, qkv_two)
-    kv_two = send(qkv.at[1, :, pl.ds(dims, 2 * dims)], far.at[1], partner)
+    kv_two = project(1, gain_two, qkv_two)
+    loads[4].wait()
     arrive(cot)
     dy_two = mm(perms[3], got[0])
     back[...] = mt(dy_two.astype(BF16), proj_two[...]).astype(BF16)
@@ -366,15 +413,13 @@
     def two(pair, carry):
         for t in range(WINDOWS):
             rows = pl.ds(t * SLOT, SLOT)
-            backward(rows, pair, *forward(1, t, pair, rows))
+            backward(1, rows, pair, *forward(1, t, pair, rows))
         return carry
 
-    lax.fori_loop(0, pairs, two, 0)
-    dkv_two = send(far_grads, got_grads.at[1], partner)
+    dkv_two = halves(two, 1)
     turned = (field[1].astype(F32) + mm(mixed[...], proj_two[...])).astype(BF16)
     result = roll(2, mm(perms[4], turned), False)
-    dkv_two.wait_recv()
-    grad_turned = finish(1, mm(perms[3], got[0]), gain_two, qkv_two)
+    grad_turned = finish(1, mm(perms[3], got[0]), gain_two, qkv_two, dkv_two)
     moved = roll(3, mm(perms[4], grad_turned), False)
     arrive(result)
     output[...] = mm(perms[6], got[2])[:plain].astype(BF16)
@@ -382,7 +427,6 @@
 
     dy_one = mm(perms[5], got[3])
     back[...] = mt(dy_one.astype(BF16), proj_one[...]).astype(BF16)
-    dkv_two.wait_send()
 
     def one_back(pair, carry):
         for t in range(WINDOWS):
@@ -391,17 +435,14 @@
             p = probs[save_at(t, pair), :]
             k = keys_of(0, rows, 0, pair)
             v = keys_of(0, rows, 1, pair)
-            backward(rows, pair, q, k, v, p, p.astype(BF16))
+            backward(0, rows, pair, q, k, v, p, p.astype(BF16))
         return carry
 
-    lax.fori_loop(0, pairs, one_back, 0)
-    dkv_one = send(far_grads, got_grads.at[0], partner)
-    dkv_one.wait_recv()
-    last_grad = finish(0, mm(perms[5], got[3]), gain_one, qkv_one)
+    dkv_one = halves(one_back, 0)
+    last_grad = finish(0, mm(perms[5], got[3]), gain_one, qkv_one, dkv_one)
     grad_stream[...] = mm(perms[7], last_grad)[:plain].astype(BF16)
     for copy in copies:
-        if copy is not dkv_two:
-            copy.wait_send()
+        copy.wait_send()
 
 
 def body(
@@ -425,13 +466,12 @@
     levels, rows, width, dims = stream.shape
     types, heads, entries = table_one.shape
     plain = levels * rows * width
-    tables = jnp.stack([table_one, table_two]).reshape(2, types * heads, entries)
-    tables = jnp.pad(tables, ((0, 0), (0, 0), (0, 128)))
     land_rows, land_cols = land_pickers()
     wide = 3 * dims
     scratch = [
         pltpu.VMEM((2, 2, types * heads * SLOT, 128), F32),
         pltpu.VMEM((WZ * WLAT * types * heads, WZ * 256), F32),
+        pltpu.VMEM((types * heads, entries), F32),
         pltpu.VMEM((types * heads * SLOT, 2 * SLOT), F32),
         pltpu.VMEM((2, ROWS, dims), BF16),
         pltpu.VMEM((2, ROWS, dims), F32),
@@ -441,44 +481,56 @@
         pltpu.VMEM((ROWS, dims), BF16),
         pltpu.VMEM((ROWS, dims), BF16),
         pltpu.VMEM((ROWS, wide), BF16),
-        pltpu.VMEM((ROWS, 2 * dims), BF16),
+        pltpu.VMEM((2, ROWS, 2 * dims), BF16),
         pltpu.VMEM((2, ROWS, 2 * dims), BF16),
         pltpu.VMEM((4, ROWS, dims), BF16),
         pltpu.VMEM((4, ROWS, dims), BF16),
-        pltpu.SemaphoreType.DMA((12,)),
-        pltpu.SemaphoreType.DMA((12,)),
+        pltpu.SemaphoreType.DMA((18,)),
+        pltpu.SemaphoreType.DMA((18,)),
+        pltpu.VMEM((dims, wide), BF16),
+        pltpu.VMEM((dims, dims), BF16),
+        pltpu.VMEM((dims, wide), BF16),
+        pltpu.VMEM((dims, dims), BF16),
+        pltpu.VMEM((WZ * 256, WIDTH * 256), BF16),
+        pltpu.SemaphoreType.DMA((5,)),
     ]
     vmem = pl.BlockSpec(memory_space=pltpu.VMEM)
+    hbm = pl.BlockSpec(memory_space=pl.ANY)
     out, grad = pl.pallas_call(
         functools.partial(kernel, lats, lons),
         out_shape=[jax.ShapeDtypeStruct((plain, dims), BF16)] * 2,
-        in_specs=[vmem] * 18,
+        in_specs=[vmem] * 6 + [hbm] * 2 + [vmem] + [hbm] * 2 + [vmem] * 4 + [hbm] + [vmem] * 3,
         out_specs=[vmem] * 2,
         scratch_shapes=scratch,
         compiler_params=pltpu.CompilerParams(
             collective_id=0, has_side_effects=True, vmem_limit_bytes=56 << 20
         ),
     )(
-        stream.reshape(plain, dims),
-        land,
-        orography,
-        land_vector.reshape(1, dims),
+        stream.transpose(0, 2, 1, 3).reshape(plain, dims),
+        land.T,
+        orography.T,
+        land_vector,
         orography_table,
-        gain_one.reshape(1, dims),
+        gain_one,
         qkv_one,
         proj_one,
-        gain_two.reshape(1, dims),
+        gain_two,
         qkv_two,
         proj_two,
-        tables,
-        cotangent.reshape(plain, dims),
+        table_one.transpose(1, 0, 2),
+        table_two.transpose(1, 0, 2),
+        cotangent.transpose(0, 2, 1, 3).reshape(plain, dims),
         jnp.asarray(permutations()),
         jnp.asarray(pickers()),
         jnp.asarray(key_rows()),
         jnp.asarray(land_rows),
         jnp.asarray(land_cols),
     )
-    return out.reshape(stream.shape), grad.reshape(stream.shape)
+
+    def placed(tokens):
+        return tokens.reshape(levels, width, rows, dims).transpose(0, 2, 1, 3)
+
+    return placed(out), placed(grad)
 
 
 def solution(mesh):

time: 67.6 us -> 50.2 us (0.74)
  Pallas kernels: 55.7 us -> 46.1 us
  local copies, waits for them, and re-layouts: 10 us -> 3.27 us
  other arithmetic: 0.9 us -> 0 us
    pallas_call x1, Pallas kernels: 55.7 us -> 46.1 us  [body(): pl.pallas_call(functools.partial(kernel, lats, lons), out_shape=[jax.Shap...]
    reshape x7 -> x0, local copies, waits for them, and re-layouts: 5.61 us -> none  [the longest x2 2.09 us: body(): return (out.reshape(stream.shape), grad.reshape(stream.shape))]
    another operation x1 -> x0, other arithmetic: 0.9 us -> none  [body(): jnp.stack([table_one, table_two]).reshape(2, types * heads, entries)]
    unnamed x24 -> x2, local copies, waits for them, and re-layouts: 4.15 us -> 3.27 us
where the time goes in v2:
time: 50.2 us; the launch traced here: 50 us
  Pallas kernels  46.1 us (92%)
  local copies, waits for them, and re-layouts  3.27 us (7%)
  between operations  0.64 us (1%)
    pallas_call x1, Pallas kernels, body(): pl.pallas_call(functools.partial(kernel, lats, lons), out_shape=[jax.Shap...  46.1 us
    unnamed x2, local copies, waits for them, and re-layouts  3.27 us

profile of v2, /device:TPU:1, one launch (start us, length us, event | category | flops | bytes accessed | tf_op | source)
XLA Modules:
  0.0 50.0 jit_solution(803430865249520309)
XLA Ops:
  0.6 46.1 %shard_map.194 = (bf16[144,768]{1,0:T(8,128)(2,1)}, bf16[144,768]{1,0:T(8,128)(2,1)}) custom-call(bf16[144,768]{1,0:T(8,128)(2,1)} %bitcast.18, s32[3,24]{1,0:T(4,128)} %bitcast.22, s32[3,24]{1,0:T(4,128)} %bitcast.23, f32[768]{0:T(1024)} %land_vector.1, f32[8,768]{1,0:T(8,128)} %orography_table.1, f32[768]{0:T(1024)} %gain_one.1, ...), custom_call_target="tpu_custom_call" | custom-call | tf_op jit(solution)/shard_map/pallas_call | solution.py:499
  46.7 1.6 %copy.23 = bf16[2,24,3,768]{3,1,2,0:T(8,128)(2,1)} copy(bf16[2,24,3,768]{3,1,2,0:T(8,128)(2,1)} %bitcast.21) | data formatting | bytes 442368
  48.3 1.6 %copy.24 = bf16[2,24,3,768]{3,1,2,0:T(8,128)(2,1)} copy(bf16[2,24,3,768]{3,1,2,0:T(8,128)(2,1)} %bitcast.20) | data formatting | bytes 442368

commit v3 on v2

--- a/solution.py
+++ b/solution.py
@@ -19,6 +19,7 @@
 TOKENS = WZ * WLAT * WIDTH
 SLOT = 80
 ROWS = WINDOWS * SLOT
+GROUPS = 3
 MAIN = 112
 STEP = 2 * WLON - 1
 RUN = WLAT * STEP
@@ -134,9 +135,9 @@
     gain_two,
     hbm_qkv_two,
     hbm_proj_two,
-    table_one,
-    table_two,
-    cotangent,
+    hbm_table_one,
+    hbm_table_two,
+    hbm_cotangent,
     perms,
     hbm_picks,
     keys_row,
@@ -167,6 +168,9 @@
     qkv_two,
     proj_two,
     pick,
+    table_one,
+    table_two,
+    cotangent,
     load_sem,
 ):
     dims = stream.shape[1]
@@ -186,6 +190,9 @@
     for source, target in (
         (hbm_qkv_one, qkv_one),
         (hbm_picks.at[parity], pick),
+        (hbm_cotangent, cotangent),
+        (hbm_table_one, table_one),
+        (hbm_table_two, table_two),
         (hbm_proj_one, proj_one),
         (hbm_qkv_two, qkv_two),
         (hbm_proj_two, proj_two),
@@ -251,7 +258,7 @@
         normed[b] = norm
         inverse[b] = inv
         h = (norm * gain[...].reshape(1, dims)).astype(BF16)
-        loads[0 if b == 0 else 3].wait()
+        loads[0 if b == 0 else 6].wait()
         for part in (1, 2):
             cols = slice(part * dims, (part + 1) * dims)
             qkv[b, :, cols] = mm(h, weight[:, cols]).astype(BF16)
@@ -262,6 +269,7 @@
         return copy
 
     kv_one = project(0, gain_one, qkv_one)
+    loads[2].wait()
     cot = roll(0, mm(perms[1, :, :plain], cotangent[...]), True)
 
     loads[1].wait()
@@ -271,6 +279,7 @@
     late = lax.broadcasted_iota(jnp.int32, (count, 256), 0) % WINDOWS == WINDOWS - 1
 
     def expand(b):
+        loads[3 + b].wait()
         for n in range(heads):
             entries[n * WINDOWS : (n + 1) * WINDOWS, :] = tables[b][n].astype(F32)
         for za in range(WZ):
@@ -359,10 +368,11 @@
     def save_at(t, pair):
         return pl.ds(pl.multiple_of((t * heads + 2 * pair) * SLOT, SLOT), 2 * SLOT)
 
-    def halves(body, b):
+    def grouped(body, b):
         sends = []
-        cut = pairs // 2
-        for first, last_pair in ((0, cut), (cut, pairs)):
+        step = pairs // GROUPS
+        for first in range(0, pairs, step):
+            last_pair = first + step
             lax.fori_loop(first, last_pair, body, 0, unroll=True)
             for part in range(2):
                 cols = pl.ds(part * dims + first * 128, (last_pair - first) * 128)
@@ -396,7 +406,7 @@
         return carry
 
     lax.fori_loop(0, pairs, one, 0, unroll=True)
-    loads[2].wait()
+    loads[5].wait()
     middle = (field[0].astype(F32) + mm(mixed[...], proj_one[...])).astype(BF16)
     moved = roll(1, mm(perms[2], middle), True)
     expand(1)
@@ -404,7 +414,7 @@
     field[1] = mm(perms[3], got[1]).astype(BF16)
 
     kv_two = project(1, gain_two, qkv_two)
-    loads[4].wait()
+    loads[7].wait()
     arrive(cot)
     dy_two = mm(perms[3], got[0])
     back[...] = mt(dy_two.astype(BF16), proj_two[...]).astype(BF16)
@@ -416,13 +426,11 @@
             backward(1, rows, pair, *forward(1, t, pair, rows))
         return carry
 
-    dkv_two = halves(two, 1)
+    dkv_two = grouped(two, 1)
+    grad_turned = finish(1, mm(perms[3], got[0]), gain_two, qkv_two, dkv_two)
+    moved = roll(3, mm(perms[4], grad_turned), False)
     turned = (field[1].astype(F32) + mm(mixed[...], proj_two[...])).astype(BF16)
     result = roll(2, mm(perms[4], turned), False)
-    grad_turned = finish(1, mm(perms[3], got[0]), gain_two, qkv_two, dkv_two)
-    moved = roll(3, mm(perms[4], grad_turned), False)
-    arrive(result)
-    output[...] = mm(perms[6], got[2])[:plain].astype(BF16)
     arrive(moved)
 
     dy_one = mm(perms[5], got[3])
@@ -438,11 +446,28 @@
             backward(0, rows, pair, q, k, v, p, p.astype(BF16))
         return carry
 
-    dkv_one = halves(one_back, 0)
+    dkv_one = grouped(one_back, 0)
+    arrive(result)
+    output[...] = mm(perms[6], got[2])[:plain].astype(BF16)
     last_grad = finish(0, mm(perms[5], got[3]), gain_one, qkv_one, dkv_one)
     grad_stream[...] = mm(perms[7], last_grad)[:plain].astype(BF16)
     for copy in copies:
         copy.wait_send()
+
+
+def hand_over(first, second, first_out, second_out, sem):
+    copies = []
+    for source, target in ((first, first_out), (second, second_out)):
+        step = source.shape[0] // 3
+        for n in range(3):
+            rows = pl.ds(n * step, step)
+            copies.append(
+                pltpu.make_async_copy(source.at[rows], target.at[rows], sem.at[len(copies)])
+            )
+    for copy in copies:
+        copy.start()
+    for copy in copies:
+        copy.wait()
 
 
 def body(
@@ -485,21 +510,24 @@
         pltpu.VMEM((2, ROWS, 2 * dims), BF16),
         pltpu.VMEM((4, ROWS, dims), BF16),
         pltpu.VMEM((4, ROWS, dims), BF16),
-        pltpu.SemaphoreType.DMA((18,)),
-        pltpu.SemaphoreType.DMA((18,)),
+        pltpu.SemaphoreType.DMA((22,)),
+        pltpu.SemaphoreType.DMA((22,)),
         pltpu.VMEM((dims, wide), BF16),
         pltpu.VMEM((dims, dims), BF16),
         pltpu.VMEM((dims, wide), BF16),
         pltpu.VMEM((dims, dims), BF16),
         pltpu.VMEM((WZ * 256, WIDTH * 256), BF16),
-        pltpu.SemaphoreType.DMA((5,)),
+        pltpu.VMEM((heads, types, entries), BF16),
+        pltpu.VMEM((heads, types, entries), BF16),
+        pltpu.VMEM((plain, dims), BF16),
+        pltpu.SemaphoreType.DMA((8,)),
     ]
     vmem = pl.BlockSpec(memory_space=pltpu.VMEM)
     hbm = pl.BlockSpec(memory_space=pl.ANY)
     out, grad = pl.pallas_call(
         functools.partial(kernel, lats, lons),
         out_shape=[jax.ShapeDtypeStruct((plain, dims), BF16)] * 2,
-        in_specs=[vmem] * 6 + [hbm] * 2 + [vmem] + [hbm] * 2 + [vmem] * 4 + [hbm] + [vmem] * 3,
+        in_specs=[vmem] * 6 + [hbm] * 2 + [vmem] + [hbm] * 5 + [vmem] + [hbm] + [vmem] * 3,
         out_specs=[vmem] * 2,
         scratch_shapes=scratch,
         compiler_params=pltpu.CompilerParams(
@@ -527,6 +555,15 @@
         jnp.asarray(land_cols),
     )
 
+    out, grad = pl.pallas_call(
+        hand_over,
+        out_shape=[jax.ShapeDtypeStruct((plain, dims), BF16)] * 2,
+        in_specs=[hbm] * 2,
+        out_specs=[hbm] * 2,
+        scratch_shapes=[pltpu.SemaphoreType.DMA((6,))],
+        compiler_params=pltpu.CompilerParams(vmem_limit_bytes=62 << 20),
+    )(out, grad)
+
     def placed(tokens):
         return tokens.reshape(levels, width, rows, dims).transpose(0, 2, 1, 3)
 

time: 50.2 us -> 62.8 us (1.25)
  Pallas kernels: 46.1 us -> 61.8 us
  local copies, waits for them, and re-layouts: 3.27 us -> 0 us
    pallas_call x0 -> x1, Pallas kernels: none -> 14.6 us  [body(): pl.pallas_call(hand_over, out_shape=[jax.ShapeDtypeStruct((plain, dims),...]
    unnamed x2 -> x0, local copies, waits for them, and re-layouts: 3.27 us -> none
    pallas_call x1, Pallas kernels: 46.1 us -> 47.2 us  [body(): pl.pallas_call(functools.partial(kernel, lats, lons), out_shape=[jax.Shap...]
where the time goes in v3:
time: 62.8 us; the launch traced here: 62.6 us
  Pallas kernels  61.8 us (98%)
  between operations  0.8 us (1%)
    pallas_call x1, Pallas kernels, body(): pl.pallas_call(functools.partial(kernel, lats, lons), out_shape=[jax.Shap...  47.2 us
    pallas_call x1, Pallas kernels, body(): pl.pallas_call(hand_over, out_shape=[jax.ShapeDtypeStruct((plain, dims),...  14.6 us

profile of v3, /device:TPU:1, one launch (start us, length us, event | category | flops | bytes accessed | tf_op | source)
XLA Modules:
  0.0 62.6 jit_solution(16217926099782703066)
XLA Ops:
  0.6 47.2 %shard_map.194 = (bf16[144,768]{1,0:T(8,128)(2,1)}, bf16[144,768]{1,0:T(8,128)(2,1)}) custom-call(bf16[144,768]{1,0:T(8,128)(2,1)} %bitcast.18, s32[3,24]{1,0:T(4,128)} %bitcast.20, s32[3,24]{1,0:T(4,128)} %bitcast.21, f32[768]{0:T(1024)} %land_vector.1, f32[8,768]{1,0:T(8,128)} %orography_table.1, f32[768]{0:T(1024)} %gain_one.1, ...), custom_call_target="tpu_custom_call" | custom-call | tf_op jit(solution)/shard_map/pallas_call | solution.py:527
  47.9 14.6 %shard_map.195 = (bf16[144,768]{1,0:T(8,128)(2,1)}, bf16[144,768]{1,0:T(8,128)(2,1)}) custom-call(bf16[144,768]{1,0:T(8,128)(2,1)} %get-tuple-element.6.first, bf16[144,768]{1,0:T(8,128)(2,1)} %get-tuple-element.7.second), custom_call_target="tpu_custom_call" | custom-call | tf_op jit(solution)/shard_map/pallas_call | solution.py:558
